TPU v7x, 256 devices: a whole 4x4x8 slice. The times are simulated.
256 devices in a mesh: lat: 4 (over x_lo, core), lon: 64 (over z, y, x_hi).
Axes of the slice: x: 4 (x_hi: 2, x_lo: 2; x = x_hi * 2 + x_lo), y: 4, z: 8, core: 2. Of those that a mesh axis runs over, the one named last changes fastest.
Arguments:
- tokens: bfloat16 [64, 1024, 1536], P('lat', 'lon'), may hold values from -6 to 6
- cotangent: bfloat16 [64, 1024, 1536], P('lat', 'lon'), may hold values from -6 to 6
- gain: float32 [1536], replicated, may hold values from 0.5 to 1.5
- w_qkv: bfloat16 [1536, 4608], P('lon'), may hold values from -0.15625 to 0.15625
- w_out: bfloat16 [1536, 1536], P('lon'), may hold values from -0.15625 to 0.15625
- logit_scale: float32 [24], replicated, may hold values from 2 to 12
- region_ids: int32 [64, 1024], P('lat', 'lon'), may hold values from 0 to 2
Outputs:
- output: bfloat16 [64, 1024, 1536], P('lat', 'lon')
- grad_input: bfloat16 [64, 1024, 1536], P('lat', 'lon')
All inputs are finite; a program needn't handle non-finite values.
Results may differ from a plain program's by a relative error of at most 0.0071.
Values may be sent and summed in bfloat16 or wider, within the bound.
No kernel may reach another device: no remote copies, remote signals or barrier semaphores. Data moves between devices by JAX's collectives and lax.ppermute only.
A program may use at most 128 MiB of HBM per device.

v0:
```python
import jax
import jax.numpy as jnp
from jax import lax
from jax.sharding import PartitionSpec as P

WIN_LAT = 4
WIN_LON = 16
SHIFT_LAT = 2
SHIFT_LON = 8


def from_behind(shard, axis, by):
    length = lax.axis_size(axis)
    return lax.ppermute(shard, axis, [(i, (i + by) % length) for i in range(length)])


def passed_along(block, axis, distance):
    devices = range(lax.axis_size(axis))
    route = [(i - distance, i) for i in devices if i - distance in devices]
    return lax.ppermute(block, axis, route)


def layer_norm(tokens_f32, gain):
    centre = tokens_f32 - jnp.mean(tokens_f32, axis=-1, keepdims=True)
    spread = jnp.mean(centre * centre, axis=-1, keepdims=True)
    return (centre * lax.rsqrt(spread + 1e-05) * gain).astype(jnp.bfloat16)


def to_windows(tensor):
    span_lat, span_lon, features = tensor.shape
    shaped = tensor.reshape(span_lat // WIN_LAT, WIN_LAT, span_lon // WIN_LON, WIN_LON, features)
    return shaped.transpose(0, 2, 1, 3, 4).reshape(-1, WIN_LAT * WIN_LON, features)


def from_windows(blocks, span_lat, span_lon):
    features = blocks.shape[-1]
    shaped = blocks.reshape(span_lat // WIN_LAT, span_lon // WIN_LON, WIN_LAT, WIN_LON, features)
    return shaped.transpose(0, 2, 1, 3, 4).reshape(span_lat, span_lon, features)


def attend_core(packed_half, region_win, valid_win, logit_scale):
    count_win, count_tok, packed_width = packed_half.shape
    heads_num = logit_scale.shape[0]
    head_size = packed_width // (3 * heads_num)
    packed_half = lax.optimization_barrier(packed_half).reshape(
        count_win, count_tok, 3, heads_num, head_size
    )
    values = packed_half[:, :, 2]
    packed = packed_half.astype(jnp.float32)
    queries = packed[:, :, 0]
    keys_all = packed[:, :, 1]
    queries = queries * lax.rsqrt(jnp.sum(queries * queries, axis=-1, keepdims=True) + 1e-06)
    keys_all = keys_all * lax.rsqrt(jnp.sum(keys_all * keys_all, axis=-1, keepdims=True) + 1e-06)
    scores = jnp.einsum("bqhe,bkhe->bhqk", queries, keys_all, precision=lax.Precision.HIGHEST)
    scores = scores * logit_scale[None, :, None, None]
    allowed = (region_win[:, :, None] == region_win[:, None, :]) & (
        valid_win[:, None, :] | jnp.eye(count_tok, dtype=bool)[None]
    )
    weights = jnp.where(allowed[:, None], jnp.exp(scores), 0.0)
    probs = (weights / jnp.sum(weights, axis=-1, keepdims=True)).astype(jnp.bfloat16)
    probs = lax.optimization_barrier(probs)
    mixed = jnp.einsum("bhqk,bkhe->bqhe", probs, values, preferred_element_type=jnp.float32)
    return mixed.reshape(count_win, count_tok, heads_num * head_size).astype(jnp.bfloat16)


def window_attend(blocks, region_win, valid_win, w_qkv, logit_scale):
    count_win, count_tok, model_dim = blocks.shape
    packed_half = jnp.dot(
        blocks.reshape(-1, model_dim), w_qkv, preferred_element_type=jnp.float32
    ).astype(jnp.bfloat16)
    packed_half = packed_half.reshape(count_win, count_tok, w_qkv.shape[1])
    return attend_core(packed_half, region_win, valid_win, logit_scale)


def project(mixed, w_out):
    leading = mixed.shape[:-1]
    result = jnp.dot(mixed.reshape(-1, mixed.shape[-1]), w_out, preferred_element_type=jnp.float32)
    return result.astype(jnp.bfloat16).reshape(leading + (w_out.shape[1],))


def project_back(upstream, w_out):
    leading = upstream.shape[:-1]
    result = lax.dot_general(
        upstream.reshape(-1, upstream.shape[-1]),
        w_out,
        (((1,), (1,)), ((), ())),
        preferred_element_type=jnp.float32,
    )
    return result.astype(jnp.bfloat16).reshape(leading + (w_out.shape[0],))


def pull_ahead(tensor):
    edge_cols = from_behind(tensor[:, :SHIFT_LON], "lon", -1)
    widened = jnp.concatenate([tensor[:, SHIFT_LON:], edge_cols], axis=1)
    rim_rows = passed_along(widened[:SHIFT_LAT], "lat", -1)
    return jnp.concatenate([widened[SHIFT_LAT:], rim_rows], axis=0)


def pull_behind(tensor):
    edge_cols = from_behind(tensor[:, -SHIFT_LON:], "lon", 1)
    widened = jnp.concatenate([edge_cols, tensor[:, :-SHIFT_LON]], axis=1)
    rim_rows = passed_along(widened[-SHIFT_LAT:], "lat", 1)
    return jnp.concatenate([rim_rows, widened[:-SHIFT_LAT]], axis=0)


def body(tokens, cotangent, gain, w_qkv, w_out, logit_scale, region_ids):
    span_lat, span_lon, model_dim = tokens.shape
    total_lat = span_lat * lax.axis_size("lat")
    full_qkv, full_out = (
        lax.all_gather(w_qkv, "lon", axis=0, tiled=True),
        lax.all_gather(w_out, "lon", axis=0, tiled=True),
    )
    tokens_f32 = tokens.astype(jnp.float32)
    normed, norm_back = jax.vjp(lambda inner: layer_norm(inner, gain), tokens_f32)
    shifted = pull_ahead(normed)
    row_index = lax.axis_index("lat") * span_lat + lax.broadcasted_iota(
        jnp.int32, (span_lat, span_lon, 1), 0
    )
    valid_win = to_windows(row_index + SHIFT_LAT < total_lat)[..., 0]
    region_win = to_windows(region_ids[..., None])[..., 0]
    blocks = to_windows(shifted)
    attended, attend_back = jax.vjp(
        lambda inner: window_attend(inner, region_win, valid_win, full_qkv, logit_scale), blocks
    )
    projected = project(attended, full_out)
    update = pull_behind(from_windows(projected, span_lat, span_lon))
    update = lax.optimization_barrier(update)
    output = (tokens_f32 + update.astype(jnp.float32)).astype(jnp.bfloat16)
    upstream_z = pull_ahead(cotangent)
    grad_mixed = project_back(to_windows(upstream_z), full_out)
    (grad_win,) = attend_back(grad_mixed)
    grad_normed = pull_behind(from_windows(grad_win, span_lat, span_lon))
    (grad_tokens,) = norm_back(grad_normed)
    grad_input = (grad_tokens + cotangent.astype(jnp.float32)).astype(jnp.bfloat16)
    return (output, grad_input)


def solution(mesh):
    return jax.shard_map(
        body,
        mesh=mesh,
        in_specs=(
            P("lat", "lon", None),
            P("lat", "lon", None),
            P(),
            P("lon", None),
            P("lon", None),
            P(),
            P("lat", "lon"),
        ),
        out_specs=(P("lat", "lon", None), P("lat", "lon", None)),
        check_vma=False,
    )
```

profile of v0, /device:TPU:1, one launch (start us, length us, event | category | flops | bytes accessed | tf_op | source)
XLA Modules:
  0.0 472.7 jit_solution(14091211622494041632)
XLA Ops:
  13.0 11.4 %collective-permute-start = (bf16[16,8,1536]{2,1,0:T(8,128)(2,1)S(1)}, bf16[16,8,1536]{2,1,0:T(8,128)(2,1)S(1)}, u32[]{:S(2)}, u32[]{:S(2)}) collective-permute-start(bf16[16,8,1536]{2,1,0:T(8,128)(2,1)S(1)} %get-tuple-element.19), channel_id=1, source_target_pairs={{0,63},{1,0},{2,1},{3,2},{4,3},{5,4},{6,5},{7,6},{8,7},{9,8},{10,9... | collective-permute-start | bytes 1179656 | tf_op jit(solution)/shard_map/ppermute | solution.py:14
  25.2 7.3 %collective-permute-done = bf16[16,8,1536]{2,1,0:T(8,128)(2,1)S(1)} collective-permute-done((bf16[16,8,1536]{2,1,0:T(8,128)(2,1)S(1)}, bf16[16,8,1536]{2,1,0:T(8,128)(2,1)S(1)}, u32[]{:S(2)}, u32[]{:S(2)}) %collective-permute-start) | collective-permute-done | bytes 393248 | tf_op jit(solution)/shard_map/ppermute | solution.py:14
  32.5 4.7 collective-permute-start.1
  37.1 4.3 collective-permute-done.4
  41.4 3.5 collective-permute-start.5
  45.2 2.7 collective-permute-done.5
  47.9 98.8 %all-gather.5.cloned.1.call-done = bf16[1536,1536]{1,0:T(8,128)(2,1)} async-done(((bf16[24,1536]{1,0:T(8,128)(2,1)}), bf16[1536,1536]{1,0:T(8,128)(2,1)}) %all-gather.5.cloned.1.call-update) | async-done | bytes 4718608 | tf_op jit(solution)/shard_map/all_gather | solution.py:111
  146.7 3.7 convolution_convert_fusion.2
  151.4 1.8 copy.25
  153.3 186.9 %all-gather.3.cloned.1.call-done = bf16[1536,4608]{1,0:T(8,128)(2,1)} async-done(((bf16[24,4608]{1,0:T(8,128)(2,1)}), bf16[1536,4608]{1,0:T(8,128)(2,1)}) %all-gather.3.cloned.1.call-update) | async-done | bytes 14155792 | tf_op jit(solution)/shard_map/all_gather | solution.py:110
  340.1 10.1 %convolution_convert_fusion = bf16[256,4608]{1,0:T(8,128)(2,1)} fusion(bf16[256,1536]{1,0:T(8,128)(2,1)S(1)} %bitcast.93, bf16[1536,4608]{1,0:T(8,128)(2,1)} %all-gather.3.cloned.1.call-done), kind=kOutput, calls=%fused_computation.1 | convolution fusion | flops 3625058304 | bytes 17301504 | tf_op jit(solution)/shard_map/jvp()/dot_general | solution.py:68
  350.2 6.9 %reshape.127 = bf16[4,64,3,24,64]{4,3,2,1,0:T(8,128)(2,1)} reshape(bf16[4,64,4608]{2,1,0:T(8,128)(2,1)} %bitcast.92) | data formatting | bytes 4718592 | tf_op jit(solution)/shard_map/jvp()/reshape | solution.py:45
  357.2 7.5 %copy.19 = bf16[4,64,3,24,64]{1,4,3,0,2:T(8,128)(2,1)} copy(bf16[4,64,3,24,64]{4,3,2,1,0:T(8,128)(2,1)} %reshape.127) | data formatting | bytes 4718592 | tf_op jit(solution)/shard_map/jvp()/reshape | solution.py:45
  364.7 3.7 convert_element_type.69
  372.1 5.4 %fusion.23 = (f32[4,24,64]{2,1,0:T(8,128)S(1)}, f32[4,24,64,64]{2,3,1,0:T(8,128)S(1)}) fusion(f32[24]{0:T(128)S(1)} %copy-done.26, pred[4,64,64]{1,2,0:T(8,128)(4,1)S(1)} %or_and_fusion, f32[4,64,3,24,64]{1,4,3,0,2:T(8,128)S(1)} %convert_element_type.69, f32[4,64,24]{1,2,0:T(8,128)S(1)} %add_rsqrt_fusion, f32[4,64,24]{1,2,0:T(8,128)S(1)} %add_rsqrt_fusion.1), kind=kOutput, calls=%fused_computation.46 | convolution fusion | flops 303949824 | bytes 8020480 | tf_op jit(solution)/shard_map/jvp(bqhe,bkhe->bhqk)/dot_general | solution.py:54
  379.8 1.7 fusion.35
  381.6 2.2 fusion.36
  383.7 2.8 copy.24
  386.5 3.4 convert_element_type.73
  390.0 4.1 convolution_convert_fusion.3
  395.4 6.8 %fusion.11 = f32[4,24,64,64]{2,3,1,0:T(8,128)S(1)} fusion(f32[4,64,3,24,64]{1,4,3,0,2:T(8,128)} %copy-done, f32[4,64,24]{1,2,0:T(8,128)S(1)} %copy-done.12, bf16[4,24,64,64]{2,3,1,0:T(8,128)(2,1)S(1)} %copy-done.5, f32[4,24,64,64]{2,3,1,0:T(8,128)S(1)} %get-tuple-element.21, f32[4,24,64]{2,1,0:T(8,128)S(1)} %copy-done.24, f32[4,24,64]{2,1,0:T(8,128)S(1)} %copy-done.14, ...), kind=kOutput, calls=%fused_computation.27 | convolution fusion | flops 305135616 | bytes 7168096 | tf_op jit(solution)/shard_map/transpose(jvp(bqhe,bkhe->bhqk))/dot_general | solution.py:54
  402.2 8.4 %fusion.10 = (f32[4,64,24]{1,2,0:T(8,128)S(1)}, f32[4,64,24]{1,2,0:T(8,128)S(1)}, f32[4,24,64,64]{2,3,1,0:T(8,128)}) fusion(f32[4,64,3,24,64]{1,4,3,0,2:T(8,128)S(1)} %bitcast.89, f32[4,24,64,64]{2,3,1,0:T(8,128)S(1)} %fusion.11, f32[4,64,24]{1,2,0:T(8,128)S(1)} %copy-done.10, bf16[4,24,64,64]{2,3,1,0:T(8,128)(2,1)S(1)} %copy-done.5, ...), kind=kOutput, calls=%fused_computation.22 | convolution fusion | flops 306696192 | bytes 10362976 | tf_op jit(solution)/shard_map/transpose(jvp(bqhe,bkhe->bhqk))/dot_general | solution.py:54
  410.7 5.3 %fusion.7 = (f32[4,64,1,24,64]{1,4,3,0,2:T(8,128)S(1)}, f32[4,64,1,24,64]{1,4,3,0,2:T(8,128)S(1)}) fusion(f32[4,24,64,64]{2,3,1,0:T(8,128)} %get-tuple-element.22, f32[4,64,3,24,64]{1,4,3,0,2:T(8,128)S(1)} %bitcast.89, f32[4,64,24]{1,2,0:T(8,128)S(1)} %get-tuple-element.24, f32[4,64,24]{1,2,0:T(8,128)} %copy-done.11, f32[4,64,24]{1,2,0:T(8,128)S(1)} %get-tuple-element.23, ...), kind=kLoop, calls=%fused_computation.13 | loop fusion | flops 3145728 | bytes 9535488 | tf_op jit(solution)/shard_map/transpose(jvp())/broadcast_in_dim | solution.py:51
  415.9 4.0 fusion
  419.9 7.0 %copy.32 = bf16[4,64,3,24,64]{4,3,2,1,0:T(8,128)(2,1)} copy(bf16[4,64,3,24,64]{1,4,3,0,2:T(8,128)(2,1)} %fusion) | data formatting | bytes 4718592 | tf_op jit(solution)/shard_map/transpose(jvp())/add_any | solution.py:48
  426.9 6.1 %reshape.129 = bf16[4,64,4608]{2,1,0:T(8,128)(2,1)S(1)} reshape(bf16[4,64,3,24,64]{4,3,2,1,0:T(8,128)(2,1)} %copy.32) | data formatting | bytes 4718592 | tf_op jit(solution)/shard_map/transpose(jvp())/reshape | solution.py:45
  433.1 7.2 %convolution_convert_fusion.1 = bf16[256,1536]{1,0:T(8,128)(2,1)S(1)} fusion(bf16[256,4608]{1,0:T(8,128)(2,1)S(1)} %bitcast.91, bf16[1536,4608]{1,0:T(8,128)(2,1)} %all-gather.3.cloned.1.call-done), kind=kOutput, calls=%fused_computation.35 | convolution fusion | flops 3624271872 | bytes 17301504 | tf_op jit(solution)/shard_map/transpose(jvp())/dot_general | solution.py:68
  440.3 3.4 collective-permute-start.6
  444.6 3.9 collective-permute-start.3
  448.4 6.8 %collective-permute-done.6 = bf16[16,8,1536]{2,1,0:T(8,128)(2,1)S(1)} collective-permute-done((bf16[16,8,1536]{2,1,0:T(8,128)(2,1)S(1)}, bf16[16,8,1536]{2,1,0:T(8,128)(2,1)S(1)}, u32[]{:S(2)}, u32[]{:S(2)}) %collective-permute-start.6) | collective-permute-done | bytes 393248 | tf_op jit(solution)/shard_map/ppermute | solution.py:14
  455.3 5.8 %collective-permute-start.7 = (bf16[2,16,1536]{2,1,0:T(8,128)(2,1)S(1)}, bf16[2,16,1536]{2,1,0:T(8,128)(2,1)S(1)}, u32[]{:S(2)}, u32[]{:S(2)}) collective-permute-start(bf16[2,16,1536]{2,1,0:T(8,128)(2,1)S(1)} %pad_maximum_fusion.4), channel_id=1, source_target_pairs={{0,64},{64,128},{128,192},{1,65},{65,129},{129,193},{2,66},{66,130... | collective-permute-start | bytes 294920 | tf_op jit(solution)/shard_map/ppermute | solution.py:20
  463.7 1.9 add_convert_fusion.1
  (110 shorter events, 18.5 us)
Async XLA Ops:
  7.2 17.2 %copy-start.7 = (bf16[16,16,1536]{2,1,0:T(8,128)(2,1)S(1)}, bf16[16,16,1536]{2,1,0:T(8,128)(2,1)}, u32[]{:S(2)}) copy-start(bf16[16,16,1536]{2,1,0:T(8,128)(2,1)} %param.8) | copy-start | bytes 2359300
  7.2 139.5 %all-gather.5.cloned.1.call-start = ((), (), s32[]{:S(2)}) async-start(), calls=%async_computation.1 | async-start | bytes 4792320 | tf_op jit(solution)/shard_map/all_gather | solution.py:111
  7.9 332.2 %all-gather.3.cloned.1.call-start = ((), (), s32[]{:S(2)}) async-start(), calls=%async_computation | async-start | bytes 14376960 | tf_op jit(solution)/shard_map/all_gather | solution.py:110
  8.7 16.3 %copy-start.25 = (s32[16,16]{1,0:T(8,128)S(1)}, s32[16,16]{1,0:T(8,128)}, u32[]{:S(2)}) copy-start(s32[16,16]{1,0:T(8,128)} %param.13) | copy-start | bytes 3076
  13.0 19.4 %collective-permute-start = (bf16[16,8,1536]{2,1,0:T(8,128)(2,1)S(1)}, bf16[16,8,1536]{2,1,0:T(8,128)(2,1)S(1)}, u32[]{:S(2)}, u32[]{:S(2)}) collective-permute-start(bf16[16,8,1536]{2,1,0:T(8,128)(2,1)S(1)} %get-tuple-element.19), channel_id=1, source_target_pairs={{0,63},{1,0},{2,1},{3,2},{4,3},{5,4},{6,5},{7,6},{8,7},{9,8},{10,9... | collective-permute-start | bytes 1179656 | tf_op jit(solution)/shard_map/ppermute | solution.py:14
  24.5 17.0 %collective-permute-start.4 = (bf16[16,8,1536]{2,1,0:T(8,128)(2,1)S(1)}, bf16[16,8,1536]{2,1,0:T(8,128)(2,1)S(1)}, u32[]{:S(2)}, u32[]{:S(2)}) collective-permute-start(bf16[16,8,1536]{2,1,0:T(8,128)(2,1)S(1)} %get-tuple-element.15), channel_id=1, source_target_pairs={{0,63},{1,0},{2,1},{3,2},{4,3},{5,4},{6,5},{7,6},{8,7},{9,8},{10,9... | collective-permute-start | bytes 1179656 | tf_op jit(solution)/shard_map/ppermute | solution.py:14
  25.2 352.4 %copy-start.19 = (pred[4,64,64]{1,2,0:T(8,128)(4,1)}, pred[4,64,64]{1,2,0:T(8,128)(4,1)S(1)}, u32[]{:S(2)}) copy-start(pred[4,64,64]{1,2,0:T(8,128)(4,1)S(1)} %or_and_fusion) | copy-start | bytes 49156
  32.5 12.7 %collective-permute-start.1 = (bf16[2,16,1536]{2,1,0:T(8,128)(2,1)S(1)}, bf16[2,16,1536]{2,1,0:T(8,128)(2,1)S(1)}, u32[]{:S(2)}, u32[]{:S(2)}) collective-permute-start(bf16[2,16,1536]{2,1,0:T(8,128)(2,1)S(1)} %pad_maximum_fusion.7), channel_id=1, source_target_pairs={{64,0},{128,64},{192,128},{65,1},{129,65},{193,129},{66,2},{130,66... | collective-permute-start | bytes 294920 | tf_op jit(solution)/shard_map/ppermute | solution.py:20
  41.4 6.4 %collective-permute-start.5 = (bf16[2,16,1536]{2,1,0:T(8,128)(2,1)S(1)}, bf16[2,16,1536]{2,1,0:T(8,128)(2,1)S(1)}, u32[]{:S(2)}, u32[]{:S(2)}) collective-permute-start(bf16[2,16,1536]{2,1,0:T(8,128)(2,1)S(1)} %pad_maximum_fusion.5), channel_id=1, source_target_pairs={{64,0},{128,64},{192,128},{65,1},{129,65},{193,129},{66,2},{130,66... | collective-permute-start | bytes 294920 | tf_op jit(solution)/shard_map/ppermute | solution.py:20
  369.5 8.1 %copy-start.4 = (bf16[4,24,64,64]{2,3,1,0:T(8,128)(2,1)}, bf16[4,24,64,64]{2,3,1,0:T(8,128)(2,1)S(1)}, u32[]{:S(2)}) copy-start(bf16[4,24,64,64]{2,3,1,0:T(8,128)(2,1)S(1)} %convolution_convert_fusion.5) | copy-start | bytes 2359300
  370.7 6.8 %copy-start.9 = (f32[4,64,24]{1,2,0:T(8,128)}, f32[4,64,24]{1,2,0:T(8,128)S(1)}, u32[]{:S(2)}) copy-start(f32[4,64,24]{1,2,0:T(8,128)S(1)} %add_rsqrt_fusion.1) | copy-start | bytes 73732
  389.9 5.4 %copy-start.5 = (bf16[4,24,64,64]{2,3,1,0:T(8,128)(2,1)S(1)}, bf16[4,24,64,64]{2,3,1,0:T(8,128)(2,1)}, u32[]{:S(2)}) copy-start(bf16[4,24,64,64]{2,3,1,0:T(8,128)(2,1)} %copy-done.4) | copy-start | bytes 2359300
  389.9 5.4 %copy-start.12 = (f32[4,64,24]{1,2,0:T(8,128)S(1)}, f32[4,64,24]{1,2,0:T(8,128)}, u32[]{:S(2)}) copy-start(f32[4,64,24]{1,2,0:T(8,128)} %copy-done.11) | copy-start | bytes 73732
  389.9 5.4 %copy-start.14 = (f32[4,24,64]{2,1,0:T(8,128)S(1)}, f32[4,24,64]{2,1,0:T(8,128)}, u32[]{:S(2)}) copy-start(f32[4,24,64]{2,1,0:T(8,128)} %copy-done.13) | copy-start | bytes 73732
  389.9 5.4 %copy-start.20 = (pred[4,64,64]{1,2,0:T(8,128)(4,1)S(1)}, pred[4,64,64]{1,2,0:T(8,128)(4,1)}, u32[]{:S(2)}) copy-start(pred[4,64,64]{1,2,0:T(8,128)(4,1)} %copy-done.19) | copy-start | bytes 49156
  389.9 5.4 %copy-start.24 = (f32[4,24,64]{2,1,0:T(8,128)S(1)}, f32[4,24,64]{2,1,0:T(8,128)}, u32[]{:S(2)}) copy-start(f32[4,24,64]{2,1,0:T(8,128)} %neg.9) | copy-start | bytes 73732
  390.0 5.4 %copy-start.27 = (f32[24]{0:T(128)S(1)}, f32[24]{0:T(128)}, u32[]{:S(2)}) copy-start(f32[24]{0:T(128)} %param.12) | copy-start | bytes 292
  394.8 7.3 %slice-start = ((s8[9437184]{0:T(1024)(128)(4,1)}), s8[4194304]{0:T(1024)(128)(4,1)S(1)}, s32[]{:S(2)}) async-start(s8[9437184]{0:T(1024)(128)(4,1)} %bitcast.88), calls=%async_computation.2 | async-start | bytes 8388608
  394.8 7.3 %slice-start.1 = ((s8[9437184]{0:T(1024)(128)(4,1)}), s8[4194304]{0:T(1024)(128)(4,1)S(1)}, s32[]{:S(2)}) async-start(s8[9437184]{0:T(1024)(128)(4,1)} %bitcast.88), calls=%async_computation.3 | async-start | bytes 8388608
  394.8 7.3 %slice-start.2 = ((s8[9437184]{0:T(1024)(128)(4,1)}), s8[1048576]{0:T(1024)(128)(4,1)S(1)}, s32[]{:S(2)}) async-start(s8[9437184]{0:T(1024)(128)(4,1)} %bitcast.88), calls=%async_computation.4 | async-start | bytes 2097152
  394.8 7.4 %copy-start.10 = (f32[4,64,24]{1,2,0:T(8,128)S(1)}, f32[4,64,24]{1,2,0:T(8,128)}, u32[]{:S(2)}) copy-start(f32[4,64,24]{1,2,0:T(8,128)} %copy-done.9) | copy-start | bytes 73732
  394.8 48.9 %collective-permute-start.2 = (bf16[16,8,1536]{2,1,0:T(8,128)(2,1)}, bf16[16,8,1536]{2,1,0:T(8,128)(2,1)}, u32[]{:S(2)}, u32[]{:S(2)}) collective-permute-start(bf16[16,8,1536]{2,1,0:T(8,128)(2,1)} %get-tuple-element.16), channel_id=1, source_target_pairs={{0,1},{1,2},{2,3},{3,4},{4,5},{5,6},{6,7},{7,8},{8,9},{9,10},{10,1... | collective-permute-start | bytes 1179656 | tf_op jit(solution)/shard_map/ppermute | solution.py:14
  402.2 8.4 %copy-start.6 = (f32[4,24,64,64]{2,3,1,0:T(8,128)}, f32[4,24,64,64]{2,3,1,0:T(8,128)S(1)}, u32[]{:S(2)}) copy-start(f32[4,24,64,64]{2,3,1,0:T(8,128)S(1)} %fusion.11) | copy-start | bytes 4718596
  402.2 8.4 %copy-start.16 = (f32[4,64,24]{1,2,0:T(8,128)S(1)}, f32[4,64,24]{1,2,0:T(8,128)}, u32[]{:S(2)}) copy-start(f32[4,64,24]{1,2,0:T(8,128)} %copy-done.15) | copy-start | bytes 73732
  402.2 8.4 %copy-start.18 = (f32[4,64,24]{1,2,0:T(8,128)S(1)}, f32[4,64,24]{1,2,0:T(8,128)}, u32[]{:S(2)}) copy-start(f32[4,64,24]{1,2,0:T(8,128)} %copy-done.17) | copy-start | bytes 73732
  440.2 22.4 %copy-start.2 = (bf16[16,16,1536]{2,1,0:T(8,128)(2,1)S(1)}, bf16[16,16,1536]{2,1,0:T(8,128)(2,1)}, u32[]{:S(2)}) copy-start(bf16[16,16,1536]{2,1,0:T(8,128)(2,1)} %param.7) | copy-start | bytes 2359300
  440.3 22.4 %copy-start.21 = (f32[1536]{0:T(1024)S(1)}, f32[1536]{0:T(1024)}, u32[]{:S(2)}) copy-start(f32[1536]{0:T(1024)} %param.9) | copy-start | bytes 18436
  440.3 22.8 %copy-start.23 = (f32[16,16]{1,0:T(8,128)S(1)}, f32[16,16]{1,0:T(8,128)}, u32[]{:S(2)}) copy-start(f32[16,16]{1,0:T(8,128)} %copy-done.22) | copy-start | bytes 3076
  440.3 14.9 %collective-permute-start.6 = (bf16[16,8,1536]{2,1,0:T(8,128)(2,1)S(1)}, bf16[16,8,1536]{2,1,0:T(8,128)(2,1)S(1)}, u32[]{:S(2)}, u32[]{:S(2)}) collective-permute-start(bf16[16,8,1536]{2,1,0:T(8,128)(2,1)S(1)} %get-tuple-element.12), channel_id=1, source_target_pairs={{0,1},{1,2},{2,3},{3,4},{4,5},{5,6},{6,7},{7,8},{8,9},{9,10},{10,1... | collective-permute-start | bytes 1179656 | tf_op jit(solution)/shard_map/ppermute | solution.py:14
  444.6 19.2 %copy-start.8 = (bf16[16,16,1536]{2,1,0:T(8,128)(2,1)S(1)}, bf16[16,16,1536]{2,1,0:T(8,128)(2,1)}, u32[]{:S(2)}) copy-start(bf16[16,16,1536]{2,1,0:T(8,128)(2,1)} %param.8) | copy-start | bytes 2359300
  444.6 16.5 %collective-permute-start.3 = (bf16[2,16,1536]{2,1,0:T(8,128)(2,1)S(1)}, bf16[2,16,1536]{2,1,0:T(8,128)(2,1)S(1)}, u32[]{:S(2)}, u32[]{:S(2)}) collective-permute-start(bf16[2,16,1536]{2,1,0:T(8,128)(2,1)S(1)} %pad_maximum_fusion.6), channel_id=1, source_target_pairs={{0,64},{64,128},{128,192},{1,65},{65,129},{129,193},{2,66},{66,130... | collective-permute-start | bytes 294920 | tf_op jit(solution)/shard_map/ppermute | solution.py:20
  455.3 7.4 %collective-permute-start.7 = (bf16[2,16,1536]{2,1,0:T(8,128)(2,1)S(1)}, bf16[2,16,1536]{2,1,0:T(8,128)(2,1)S(1)}, u32[]{:S(2)}, u32[]{:S(2)}) collective-permute-start(bf16[2,16,1536]{2,1,0:T(8,128)(2,1)S(1)} %pad_maximum_fusion.4), channel_id=1, source_target_pairs={{0,64},{64,128},{128,192},{1,65},{65,129},{129,193},{2,66},{66,130... | collective-permute-start | bytes 294920 | tf_op jit(solution)/shard_map/ppermute | solution.py:20
  (9 other events, 23.7 us)
Sparse Core Ops, SparseCore 0:
  11.7 134.9 all-gather.4
  150.4 189.7 all-gather.2
where the time goes:
time: 480 us; the launch traced here: 473 us
  waiting for transfers between devices  309 us (64%)
  matrix products  50.5 us (11%)
  local copies, waits for them, and re-layouts  39.3 us (8%)
  starting transfers between devices  33.6 us (7%)
  other arithmetic  25.9 us (5%)
  between operations  14.9 us (3%)
    all_gather x1, waiting for transfers between devices, body(): lax.all_gather(w_qkv, 'lon', axis=0, tiled=True)  187 us
    all_gather x1, waiting for transfers between devices, body(): lax.all_gather(w_out, 'lon', axis=0, tiled=True)  98.8 us
    reshape x3, local copies, waits for them, and re-layouts, attend_core(): lax.optimization_barrier(packed_half)  20.6 us
    dot_general x3, matrix products, attend_core(): jnp.einsum('bqhe,bkhe->bhqk', queries, keys_all, precision=lax.Precision....  20.6 us
    ppermute x4, waiting for transfers between devices, from_behind(): lax.ppermute(shard, axis, [(i, (i + by) % length) for i in range(length)])  18.4 us
    ppermute x4, starting transfers between devices, passed_along(): return lax.ppermute(block, axis, route)  17.8 us
    dot_general x2, matrix products, window_attend(): jnp.dot(blocks.reshape(-1, model_dim), w_qkv, preferred_element_type=jnp....  17.3 us
    ppermute x4, starting transfers between devices, from_behind(): lax.ppermute(shard, axis, [(i, (i + by) % length) for i in range(length)])  15.6 us
  transfers between devices with their start and end apart: 10, of which 7 were waited for; matrix products, arithmetic and copies ran while one was open for 12% of the time, Pallas kernels for 0%

commit v1 on v0

v1 whole, which is shorter than its diff:
```python
import functools
import itertools

import jax
import jax.numpy as jnp
from jax import lax
from jax.experimental import pallas as pl
from jax.experimental.pallas import tpu as pltpu
from jax.sharding import Mesh
from jax.sharding import PartitionSpec as P

SHIFT_LAT = 2
SHIFT_LON = 8
D = 1536
SIZES = {"xl": 2, "core": 2, "z": 8, "y": 4, "xh": 2}
AXES = tuple(SIZES)
LAT = ("xl", "core")
LON = ("z", "y", "xh")
TOK = 256
WIN = 64
PAIRS = 12
Y_ORDER = (0, 1, -1, 2)
Z_ORDER = (0, 1, -1, 2, -2, 3, -3, 4)
UNITS = 32
UROWS = 48


def linear(place, axes):
    total = 0
    for axis in axes:
        total = total * SIZES[axis] + place[axis]
    return total


def permutation(target):
    pairs = []
    for values in itertools.product(*[range(SIZES[axis]) for axis in AXES]):
        place = dict(zip(AXES, values))
        goal = target(dict(place))
        if goal is not None:
            pairs.append((linear(place, AXES), linear(goal, AXES)))
    return pairs


def along(axis, step):
    def target(place):
        place[axis] = (place[axis] + step) % SIZES[axis]
        return place

    return permutation(target)


def across_x():
    def target(place):
        x = 3 - (place["xh"] * 2 + place["xl"])
        place["xh"], place["xl"] = x // 2, x % 2
        return place

    return permutation(target)


def send(value, pairs):
    return lax.ppermute(value, AXES, pairs)


def lon_ring(value, step):
    size = SIZES["z"] * SIZES["y"] * SIZES["xh"]
    return lax.ppermute(value, LON, [(i, (i + step) % size) for i in range(size)])


def lat_line(value, step):
    size = SIZES["xl"] * SIZES["core"]
    return lax.ppermute(
        value, LAT, [(i, i + step) for i in range(size) if 0 <= i + step < size]
    )


def both_ways(block, axis):
    size = SIZES[axis]
    got = []
    ahead = behind = block
    for step in range(1, size // 2):
        ahead = send(ahead, along(axis, 1))
        behind = send(behind, along(axis, -1))
        got += [(step, None, ahead), (-step, None, behind)]
    half = block.shape[-1] // 2
    got.append((size // 2, 0, send(ahead[..., :half], along(axis, 1))))
    got.append((size // 2, 1, send(behind[..., half:], along(axis, -1))))
    return got


def gather_weights(w_qkv, w_out):
    core = lax.axis_index("core")
    x_hi = lax.axis_index("xh")
    first = jnp.where(core == 0, w_qkv[:, :D], w_qkv[:, 2 * D :])
    second = jnp.where(core == 0, w_qkv[:, D : 2 * D], w_out)

    def cross(block):
        other = send(block, across_x())
        low = jnp.where(x_hi == 0, block, other)
        high = jnp.where(x_hi == 0, other, block)
        return jnp.concatenate([low, high])[None]

    first, second = cross(first), cross(second)
    first = jnp.concatenate([first] + [send(first, along("y", s)) for s in Y_ORDER[1:]])
    ahead = behind = second
    parts = [second]
    for _ in range(1, SIZES["z"] // 2):
        ahead = send(ahead, along("z", 1))
        behind = send(behind, along("z", -1))
        parts += [ahead, behind]
    parts.append(send(ahead, along("z", 1)))
    second = jnp.concatenate(parts)
    own = [(0, step, half, block) for step, half, block in [(0, None, first)] + both_ways(first, "z")]
    own += [(1, step, half, block) for step, half, block in [(0, None, second)] + both_ways(second, "y")]
    plan, blocks = [], []
    for kind, step, half, block in own:
        plan += [(kind, step, half, 0), (kind, step, half, 1)]
        blocks += [block, send(block, along("core", 1))]
    return plan, blocks


def pull_ahead(tensor):
    edge = lon_ring(tensor[:, :, :SHIFT_LON], -1)
    widened = jnp.concatenate([tensor[:, :, SHIFT_LON:], edge], axis=2)
    rim = lat_line(widened[:, :SHIFT_LAT], -1)
    return jnp.concatenate([widened[:, SHIFT_LAT:], rim], axis=1)


def pull_behind(tensor):
    edge = lon_ring(tensor[:, :, -SHIFT_LON:], 1)
    widened = jnp.concatenate([edge, tensor[:, :, :-SHIFT_LON]], axis=2)
    rim = lat_line(widened[:, -SHIFT_LAT:], 1)
    return jnp.concatenate([rim, widened[:, :-SHIFT_LAT]], axis=1)


def mm(a, b):
    return lax.dot_general(a, b, (((1,), (0,)), ((), ())), preferred_element_type=jnp.float32)


def mm_nt(a, b):
    return lax.dot_general(a, b, (((1,), (1,)), ((), ())), preferred_element_type=jnp.float32)


def mm_tn(a, b):
    return lax.dot_general(a, b, (((0,), (0,)), ((), ())), preferred_element_type=jnp.float32)


def bf(value):
    return value.astype(jnp.bfloat16)


def sum_heads(value, ones):
    high = bf(value)
    low = bf(value - high.astype(jnp.float32))
    return mm(high, ones) + mm(low, ones)


def window_kernel(plan, pos, xs, gs, mask, gain, scale, *refs):
    count = len(plan)
    blocks = refs[:count]
    upd, gwin = refs[count : count + 2]
    weights, normed, gatt, packed, attended, sem = refs[count + 2 :]
    z, y, core = pos[0], pos[1], pos[2]

    copies = 0
    for (kind, step, half, other), block in zip(plan, blocks):
        side = lax.rem(core + other, 2)
        matrix = 2 * side + kind
        cols = slice(None) if half is None else pl.ds(half * (D // 2), D // 2)
        for j, offset in enumerate(Y_ORDER if kind == 0 else Z_ORDER):
            dz, dy = (step, offset) if kind == 0 else (offset, step)
            unit = lax.rem(z - dz + 8, 8) * 4 + lax.rem(y - dy + 4, 4)
            pltpu.make_async_copy(block.at[j], weights.at[matrix, unit, :, cols], sem.at[copies]).start()
            copies += 1

    for i in range(4):
        rows = pl.ds(i * WIN, WIN)
        x = xs[rows, :].astype(jnp.float32)
        centre = x - jnp.mean(x, axis=-1, keepdims=True)
        spread = jnp.mean(centre * centre, axis=-1, keepdims=True)
        normed[rows, :] = bf(centre * lax.rsqrt(spread + 1e-05) * gain[...])

    copies = 0
    for (kind, step, half, other), block in zip(plan, blocks):
        cols = slice(None) if half is None else pl.ds(half * (D // 2), D // 2)
        for j in range(block.shape[0]):
            pltpu.make_async_copy(block.at[j], weights.at[0, 0, :, cols], sem.at[copies]).wait()
            copies += 1

    @pl.loop(0, 2)
    def _(i):
        w = weights[3, pl.ds(i * 16, 16)].reshape(768, D)
        gatt[:, pl.ds(pl.multiple_of(i * 768, 128), 768)] = bf(mm_nt(gs[...], w))

    @pl.loop(0, 3)
    def _(m):
        @pl.loop(0, 3)
        def _(i):
            w = weights[m, :, :, pl.ds(pl.multiple_of(i * 512, 128), 512)].reshape(D, 512)
            packed[:, pl.ds(pl.multiple_of(m * D + i * 512, 128), 512)] = bf(mm(normed[...], w))

    lane = lax.broadcasted_iota(jnp.int32, (128, 128), 1)
    row = lax.broadcasted_iota(jnp.int32, (128, 128), 0)
    same = (lane < 64) == (row < 64)
    ones = jnp.where(same, 1.0, 0.0).astype(jnp.bfloat16)
    left = lax.broadcasted_iota(jnp.int32, (WIN, 128), 1) < 64

    def spread_heads(block):
        zero = jnp.zeros_like(block)
        return jnp.concatenate([jnp.where(left, block, zero), jnp.where(left, zero, block)], axis=0)

    def fold_heads(block):
        return jnp.where(left, block[:WIN], block[WIN:])

    @pl.loop(0, PAIRS)
    def _(p):
        at_q = pl.ds(pl.multiple_of(p * 128, 128), 128)
        at_k = pl.ds(pl.multiple_of(D + p * 128, 128), 128)
        at_v = pl.ds(pl.multiple_of(2 * D + p * 128, 128), 128)
        q = packed[:, at_q].astype(jnp.float32)
        k = packed[:, at_k].astype(jnp.float32)
        rq = lax.rsqrt(sum_heads(q * q, ones) + 1e-06)
        rk = lax.rsqrt(sum_heads(k * k, ones) + 1e-06)
        qn, kn = q * rq, k * rk
        qb, kb = bf(qn), bf(kn)
        factor = scale[pl.ds(p, 1), :]
        dqs, dks = [], []
        for i in range(4):
            rows = pl.ds(i * WIN, WIN)
            part = slice(i * WIN, (i + 1) * WIN)
            k2 = spread_heads(kb[part])
            v2 = spread_heads(packed[rows, at_v])
            d_out = gatt[rows, at_q]
            weight = jnp.exp(mm_nt(qb[part], k2) * factor) * mask[rows, :]
            prob = weight / sum_heads(weight, ones)
            prob16 = bf(prob)
            attended[rows, at_q] = bf(mm(prob16, v2))
            d_prob = mm_nt(d_out, v2)
            d_score = bf(prob * (d_prob - sum_heads(prob * d_prob, ones)) * factor)
            packed[rows, at_v] = bf(fold_heads(mm_tn(prob16, d_out)))
            dqs.append(mm(d_score, k2))
            dks.append(fold_heads(mm_tn(d_score, qb[part])))
        dq = jnp.concatenate(dqs, axis=0)
        dk = jnp.concatenate(dks, axis=0)
        packed[:, at_q] = bf(rq * (dq - qn * sum_heads(qn * dq, ones)))
        packed[:, at_k] = bf(rk * (dk - kn * sum_heads(kn * dk, ones)))

    @pl.loop(0, 3)
    def _(i):
        at = pl.ds(pl.multiple_of(i * 512, 128), 512)
        upd[:, at] = bf(mm(attended[...], weights[3, :, :, at].reshape(D, 512)))

    @pl.loop(0, 2)
    def _(i):
        total = mm_nt(packed[:, :D], weights[0, pl.ds(i * 16, 16)].reshape(768, D))
        total += mm_nt(packed[:, D : 2 * D], weights[1, pl.ds(i * 16, 16)].reshape(768, D))
        total += mm_nt(packed[:, 2 * D :], weights[2, pl.ds(i * 16, 16)].reshape(768, D))
        gwin[:, pl.ds(pl.multiple_of(i * 768, 128), 768)] = bf(total)


def window_attention(pos, xs, gs, mask, gain, scale, plan, blocks):
    vmem = pl.BlockSpec(memory_space=pltpu.VMEM)
    copies = sum(block.shape[0] for block in blocks)
    return pl.pallas_call(
        functools.partial(window_kernel, plan),
        out_shape=[jax.ShapeDtypeStruct((TOK, D), jnp.bfloat16)] * 2,
        in_specs=[pl.BlockSpec(memory_space=pltpu.SMEM)]
        + [vmem] * 5
        + [pl.BlockSpec(memory_space=pl.ANY)] * len(blocks),
        out_specs=[vmem, vmem],
        scratch_shapes=[
            pltpu.VMEM((4, UNITS, UROWS, D), jnp.bfloat16),
            pltpu.VMEM((TOK, D), jnp.bfloat16),
            pltpu.VMEM((TOK, D), jnp.bfloat16),
            pltpu.VMEM((TOK, 3 * D), jnp.bfloat16),
            pltpu.VMEM((TOK, D), jnp.bfloat16),
            pltpu.SemaphoreType.DMA((copies,)),
        ],
        compiler_params=pltpu.CompilerParams(vmem_limit_bytes=56 * 1024 * 1024),
        cost_estimate=pl.CostEstimate(
            flops=11 * 10**9, bytes_accessed=24 * 10**6, transcendentals=2 * 10**6
        ),
        name="window_attention",
    )(pos, xs, gs, mask, gain, scale, *blocks)


def finish_kernel(tokens, cotangent, update, grad, gain, out, grad_in):
    for i in range(4):
        rows = pl.ds(i * WIN, WIN)
        x = tokens[rows, :].astype(jnp.float32)
        out[rows, :] = bf(x + update[rows, :].astype(jnp.float32))
        centre = x - jnp.mean(x, axis=-1, keepdims=True)
        r = lax.rsqrt(jnp.mean(centre * centre, axis=-1, keepdims=True) + 1e-05)
        unit = centre * r
        g = grad[rows, :].astype(jnp.float32) * gain[...]
        pull = g - jnp.mean(g, axis=-1, keepdims=True)
        pull -= unit * jnp.mean(g * unit, axis=-1, keepdims=True)
        grad_in[rows, :] = bf(pull * r + cotangent[rows, :].astype(jnp.float32))


def finish(tokens, cotangent, update, grad, gain):
    vmem = pl.BlockSpec(memory_space=pltpu.VMEM)
    return pl.pallas_call(
        finish_kernel,
        out_shape=[jax.ShapeDtypeStruct((TOK, D), jnp.bfloat16)] * 2,
        in_specs=[vmem] * 5,
        out_specs=[vmem, vmem],
        compiler_params=pltpu.CompilerParams(vmem_limit_bytes=32 * 1024 * 1024),
        name="finish",
    )(tokens, cotangent, update, grad, gain)


def body(tokens, cotangent, gain, w_qkv, w_out, logit_scale, region_ids):
    lat, lon, _ = tokens.shape
    plan, blocks = gather_weights(w_qkv, w_out)
    shifted = pull_ahead(jnp.stack([tokens, cotangent]))
    shifted = shifted.reshape(2, TOK, D)
    gain = gain[None]
    scale = jnp.repeat(logit_scale, 64).reshape(PAIRS, 128)
    region = region_ids.reshape(4, WIN)
    row = lax.axis_index(LAT) * lat + lax.broadcasted_iota(jnp.int32, (lat, lon), 0)
    total_lat = lat * SIZES["xl"] * SIZES["core"]
    valid = (row + SHIFT_LAT < total_lat).reshape(4, WIN)
    allowed = (region[:, :, None] == region[:, None, :]) & (
        valid[:, None, :] | jnp.eye(WIN, dtype=bool)[None]
    )
    mask = allowed.astype(jnp.float32).reshape(TOK, WIN)
    mask = jnp.concatenate([mask, mask], axis=1)
    pos = jnp.stack([lax.axis_index("z"), lax.axis_index("y"), lax.axis_index("core")]).astype(jnp.int32)
    update, grad = window_attention(pos, shifted[0], shifted[1], mask, gain, scale, plan, blocks)
    update = pull_behind(update.reshape(1, lat, lon, D)).reshape(TOK, D)
    grad = pull_behind(grad.reshape(1, lat, lon, D)).reshape(TOK, D)
    output, grad_input = finish(
        tokens.reshape(TOK, D), cotangent.reshape(TOK, D), update, grad, gain
    )
    return output.reshape(lat, lon, D), grad_input.reshape(lat, lon, D)


def solution(mesh):
    fine = Mesh(mesh.devices.reshape(tuple(SIZES.values())), AXES)
    grid = P(LAT, LON, None)
    return jax.shard_map(
        body,
        mesh=fine,
        in_specs=(grid, grid, P(), P(LON, None), P(LON, None), P(), P(LAT, LON)),
        out_specs=(grid, grid),
        check_vma=False,
    )
```

time: 480 us -> 233 us (0.49); the launches traced: 473 us -> 233 us
  waiting for transfers between devices: 309 us -> 86.6 us
  Pallas kernels: 0 us -> 56.7 us
  matrix products: 50.5 us -> 0 us
  starting transfers between devices: 33.6 us -> 74.5 us
  local copies, waits for them, and re-layouts: 39.3 us -> 7.94 us
  other arithmetic: 25.9 us -> 5.82 us
  between operations: 14.9 us -> 1.18 us
    all_gather x2 -> x0, waiting for transfers between devices: 286 us -> none  [the longest x1 187 us: body(): lax.all_gather(w_qkv, 'lon', axis=0, tiled=True)]
    ppermute x8 -> x44, waiting for transfers between devices: 21.6 us -> 86.6 us  [the longest x38 61.6 us: send(): return lax.ppermute(value, AXES, pairs)]
    pallas_call x0 -> x2, Pallas kernels: none -> 56.7 us  [the longest x1 54.7 us: window_attention(): pl.pallas_call(functools.partial(window_kernel, plan), out_shape=[jax.Sha...]
    dot_general x10 -> x0, matrix products: 50.5 us -> none  [the longest x3 20.6 us: attend_core(): jnp.einsum('bqhe,bkhe->bhqk', queries, keys_all, precision=lax.Precision....]
    ppermute x8 -> x44, starting transfers between devices: 33.5 us -> 74.5 us  [the longest x38 53.8 us: send(): return lax.ppermute(value, AXES, pairs)]
    reshape x5 -> x0, local copies, waits for them, and re-layouts: 23.4 us -> none  [the longest x3 20.6 us: attend_core(): lax.optimization_barrier(packed_half)]
    convert_element_type x3 -> x0, other arithmetic: 7.03 us -> none  [the longest x1 3.66 us: attend_core(): packed = packed_half.astype(jnp.float32)]
    add_any x1 -> x0, local copies, waits for them, and re-layouts: 6.98 us -> none  [attend_core(): values = packed_half[:, :, 2]]
  transfers between devices with their start and end apart: 10 -> 44, of which waited for: 7 -> 21; matrix products, arithmetic and copies ran while one was open for 12% -> 4% of each run, Pallas kernels for 0% -> 0%
where the time goes in v1:
time: 233 us
  waiting for transfers between devices  86.6 us (37%)
  starting transfers between devices  74.5 us (32%)
  Pallas kernels  56.7 us (24%)
  local copies, waits for them, and re-layouts  7.94 us (3%)
  other arithmetic  5.82 us (2%)
    ppermute x38, waiting for transfers between devices, send(): return lax.ppermute(value, AXES, pairs)  61.6 us
    pallas_call x1, Pallas kernels, window_attention(): pl.pallas_call(functools.partial(window_kernel, plan), out_shape=[jax.Sha...  54.7 us
    ppermute x38, starting transfers between devices, send(): return lax.ppermute(value, AXES, pairs)  53.8 us
    ppermute x3, waiting for transfers between devices, lon_ring(): lax.ppermute(value, LON, [(i, (i + step) % size) for i in range(size)])  18.8 us
    ppermute x3, starting transfers between devices, lon_ring(): lax.ppermute(value, LON, [(i, (i + step) % size) for i in range(size)])  12.3 us
    ppermute x3, starting transfers between devices, lat_line(): lax.ppermute(value, LAT, [(i, i + step) for i in range(size) if 0 <= i +...  8.41 us
    ppermute x3, waiting for transfers between devices, lat_line(): lax.ppermute(value, LAT, [(i, i + step) for i in range(size) if 0 <= i +...  6.25 us
  transfers between devices with their start and end apart: 44, of which 21 were waited for; matrix products, arithmetic and copies ran while one was open for 4% of the time, Pallas kernels for 0%

profile of v1, /device:TPU:1, one launch (start us, length us, event | category | flops | bytes accessed | tf_op | source)
XLA Modules:
  0.0 232.8 jit_solution(3666998422677119627)
XLA Ops:
  1.7 3.4 %collective-permute-start.23 = (bf16[24,1536]{1,0:T(8,128)(2,1)S(1)}, bf16[24,1536]{1,0:T(8,128)(2,1)S(1)}, u32[]{:S(2)}, u32[]{:S(2)}) collective-permute-start(bf16[24,1536]{1,0:T(8,128)(2,1)S(1)} %get-tuple-element.18), channel_id=1, source_target_pairs={{0,129},{1,128},{2,131},{3,130},{4,133},{5,132},{6,135},{7,134},{8... | collective-permute-start | bytes 221192 | tf_op jit(solution)/shard_map/ppermute | solution.py:63
  5.2 1.5 pad_maximum_fusion.3
  6.6 9.4 %collective-permute-start = (bf16[2,16,8,1536]{3,2,1,0:T(8,128)(2,1)S(1)}, bf16[2,16,8,1536]{3,2,1,0:T(8,128)(2,1)S(1)}, u32[]{:S(2)}, u32[]{:S(2)}) collective-permute-start(bf16[2,16,8,1536]{3,2,1,0:T(8,128)(2,1)S(1)} %get-tuple-element.12), channel_id=1, source_target_pairs={{0,63},{1,0},{2,1},{3,2},{4,3},{5,4},{6,5},{7,6},{8,7},{9,8},{10,9... | collective-permute-start | bytes 2359304 | tf_op jit(solution)/shard_map/ppermute | solution.py:68
  17.8 1.9 collective-permute-start.25
  19.7 2.3 collective-permute-done.5
  22.0 1.6 collective-permute-done.3
  25.2 2.3 collective-permute-done.24
  27.5 18.7 %collective-permute-start.6 = (bf16[4,48,1536]{2,1,0:T(8,128)(2,1)S(1)}, bf16[4,48,1536]{2,1,0:T(8,128)(2,1)S(1)}, u32[]{:S(2)}, u32[]{:S(2)}) collective-permute-start(bf16[4,48,1536]{2,1,0:T(8,128)(2,1)S(1)} %pad_maximum_fusion.4.refs_0_), channel_id=1, source_target_pairs={{0,64},{1,65},{2,66},{3,67},{4,68},{5,69},{6,70},{7,71},{8,72},{9,... | collective-permute-start | bytes 1769480 | tf_op jit(solution)/shard_map/ppermute | solution.py:63
  46.3 7.0 %collective-permute-done.26 = bf16[1,48,1536]{2,1,0:T(8,128)(2,1)S(1)} collective-permute-done((bf16[1,48,1536]{2,1,0:T(8,128)(2,1)S(1)}, bf16[1,48,1536]{2,1,0:T(8,128)(2,1)S(1)}, u32[]{:S(2)}, u32[]{:S(2)}) %collective-permute-start.26) | collective-permute-done | bytes 147488 | tf_op jit(solution)/shard_map/ppermute | solution.py:63
  54.2 3.4 %collective-permute-done.27 = bf16[1,48,1536]{2,1,0:T(8,128)(2,1)S(1)} collective-permute-done((bf16[1,48,1536]{2,1,0:T(8,128)(2,1)S(1)}, bf16[1,48,1536]{2,1,0:T(8,128)(2,1)S(1)}, u32[]{:S(2)}, u32[]{:S(2)}) %collective-permute-start.27) | collective-permute-done | bytes 147488 | tf_op jit(solution)/shard_map/ppermute | solution.py:63
  57.6 5.2 %collective-permute-done.28 = bf16[1,48,1536]{2,1,0:T(8,128)(2,1)S(1)} collective-permute-done((bf16[1,48,1536]{2,1,0:T(8,128)(2,1)S(1)}, bf16[1,48,1536]{2,1,0:T(8,128)(2,1)S(1)}, u32[]{:S(2)}, u32[]{:S(2)}) %collective-permute-start.28) | collective-permute-done | bytes 147488 | tf_op jit(solution)/shard_map/ppermute | solution.py:63
  63.6 3.1 %collective-permute-done.29 = bf16[1,48,1536]{2,1,0:T(8,128)(2,1)S(1)} collective-permute-done((bf16[1,48,1536]{2,1,0:T(8,128)(2,1)S(1)}, bf16[1,48,1536]{2,1,0:T(8,128)(2,1)S(1)}, u32[]{:S(2)}, u32[]{:S(2)}) %collective-permute-start.29) | collective-permute-done | bytes 147488 | tf_op jit(solution)/shard_map/ppermute | solution.py:63
  66.8 2.9 %collective-permute-start.13 = (bf16[4,48,1536]{2,1,0:T(8,128)(2,1)S(1)}, bf16[4,48,1536]{2,1,0:T(8,128)(2,1)S(1)}, u32[]{:S(2)}, u32[]{:S(2)}) collective-permute-start(bf16[4,48,1536]{2,1,0:T(8,128)(2,1)S(1)} %collective-permute-done.9.refs_4_), channel_id=1, source_target_pairs={{0,56},{1,57},{2,58},{3,59},{4,60},{5,61},{6,62},{7,63},{8,0},{9,1... | collective-permute-start | bytes 1769480 | tf_op jit(solution)/shard_map/ppermute | solution.py:63
  69.8 2.2 collective-permute-done.30
  72.0 12.1 %collective-permute-start.10 = (bf16[4,48,1536]{2,1,0:T(8,128)(2,1)S(1)}, bf16[4,48,1536]{2,1,0:T(8,128)(2,1)S(1)}, u32[]{:S(2)}, u32[]{:S(2)}) collective-permute-start(bf16[4,48,1536]{2,1,0:T(8,128)(2,1)S(1)} %collective-permute-done.9.refs_4_), channel_id=1, source_target_pairs={{0,64},{1,65},{2,66},{3,67},{4,68},{5,69},{6,70},{7,71},{8,72},{9,... | collective-permute-start | bytes 1769480 | tf_op jit(solution)/shard_map/ppermute | solution.py:63
  85.7 2.5 %collective-permute-start.1 = (bf16[2,2,16,1536]{3,2,1,0:T(8,128)(2,1)S(1)}, bf16[2,2,16,1536]{3,2,1,0:T(8,128)(2,1)S(1)}, u32[]{:S(2)}, u32[]{:S(2)}) collective-permute-start(bf16[2,2,16,1536]{3,2,1,0:T(8,128)(2,1)S(1)} %pad_maximum_fusion.5), channel_id=1, source_target_pairs={{64,0},{128,64},{192,128},{65,1},{129,65},{193,129},{66,2},{130,66... | collective-permute-start | bytes 589832 | tf_op jit(solution)/shard_map/ppermute | solution.py:73
  88.2 4.7 %collective-permute-done.1 = bf16[2,2,16,1536]{3,2,1,0:T(8,128)(2,1)S(1)} collective-permute-done((bf16[2,2,16,1536]{3,2,1,0:T(8,128)(2,1)S(1)}, bf16[2,2,16,1536]{3,2,1,0:T(8,128)(2,1)S(1)}, u32[]{:S(2)}, u32[]{:S(2)}) %collective-permute-start.1) | collective-permute-done | bytes 196640 | tf_op jit(solution)/shard_map/ppermute | solution.py:73
  93.6 13.1 %collective-permute-done.11.refs_6_ = bf16[4,48,1536]{2,1,0:T(8,128)(2,1)S(1)} collective-permute-done((bf16[4,48,1536]{2,1,0:T(8,128)(2,1)S(1)}, bf16[4,48,1536]{2,1,0:T(8,128)(2,1)S(1)}, u32[]{:S(2)}, u32[]{:S(2)}) %collective-permute-start.11) | collective-permute-done | bytes 589856 | tf_op jit(solution)/shard_map/ppermute | solution.py:63
  108.2 3.6 %collective-permute-done.34.refs_22_ = bf16[8,48,1536]{2,1,0:T(8,128)(2,1)S(1)} collective-permute-done((bf16[8,48,1536]{2,1,0:T(8,128)(2,1)S(1)}, bf16[8,48,1536]{2,1,0:T(8,128)(2,1)S(1)}, u32[]{:S(2)}, u32[]{:S(2)}) %collective-permute-start.34) | collective-permute-done | bytes 1179680 | tf_op jit(solution)/shard_map/ppermute | solution.py:63
  114.4 5.4 %collective-permute-done.17.refs_12_ = bf16[4,48,1536]{2,1,0:T(8,128)(2,1)} collective-permute-done((bf16[4,48,1536]{2,1,0:T(8,128)(2,1)S(1)}, bf16[4,48,1536]{2,1,0:T(8,128)(2,1)}, u32[]{:S(2)}, u32[]{:S(2)}) %collective-permute-start.17) | collective-permute-done | bytes 589856 | tf_op jit(solution)/shard_map/ppermute | solution.py:63
  119.8 1.6 collective-permute-start.38
  125.5 5.7 %collective-permute-done.21.refs_16_ = bf16[4,48,768]{2,1,0:T(8,128)(2,1)} collective-permute-done((bf16[4,48,768]{2,1,0:T(8,128)(2,1)S(1)}, bf16[4,48,768]{2,1,0:T(8,128)(2,1)}, u32[]{:S(2)}, u32[]{:S(2)}) %collective-permute-start.21) | collective-permute-done | bytes 294944 | tf_op jit(solution)/shard_map/ppermute | solution.py:63
  131.2 2.1 collective-permute-done.19.refs_14_
  134.3 2.7 %collective-permute-done.36.refs_24_ = bf16[8,48,768]{2,1,0:T(8,128)(2,1)} collective-permute-done((bf16[8,48,768]{2,1,0:T(8,128)(2,1)S(1)}, bf16[8,48,768]{2,1,0:T(8,128)(2,1)}, u32[]{:S(2)}, u32[]{:S(2)}) %collective-permute-start.36) | collective-permute-done | bytes 589856 | tf_op jit(solution)/shard_map/ppermute | solution.py:63
  145.4 54.7 %window_attention.1 = (bf16[256,1536]{1,0:T(8,128)(2,1)}, bf16[256,1536]{1,0:T(8,128)(2,1)}) custom-call(s32[3]{0:T(128)} %pad_add_fusion.pos, bf16[256,1536]{1,0:T(8,128)(2,1)} %bitcast.36, bf16[256,1536]{1,0:T(8,128)(2,1)} %bitcast.35, f32[256,128]{1,0:T(8,128)} %add_convert_fusion.mask, f32[1,1536]{1,0:T(1,128)} %broadcast_in_dim.17.gain, ...), custom_call_target="tpu_custom_call" | custom-call | flops 11000000512 | bytes 24000000 | tf_op jit(solution)/shard_map/window_attention/pallas_call | solution.py:265
  201.4 2.7 %collective-permute-start.40 = (bf16[1,16,8,1536]{3,2,1,0:T(8,128)(2,1)S(1)}, bf16[1,16,8,1536]{3,2,1,0:T(8,128)(2,1)S(1)}, u32[]{:S(2)}, u32[]{:S(2)}) collective-permute-start(bf16[1,16,8,1536]{3,2,1,0:T(8,128)(2,1)S(1)} %get-tuple-element.16), channel_id=1, source_target_pairs={{0,1},{1,2},{2,3},{3,4},{4,5},{5,6},{6,7},{7,8},{8,9},{9,10},{10,1... | collective-permute-start | bytes 1179656 | tf_op jit(solution)/shard_map/ppermute | solution.py:68
  204.3 13.5 %collective-permute-done.40 = bf16[1,16,8,1536]{3,2,1,0:T(8,128)(2,1)S(1)} collective-permute-done((bf16[1,16,8,1536]{3,2,1,0:T(8,128)(2,1)S(1)}, bf16[1,16,8,1536]{3,2,1,0:T(8,128)(2,1)S(1)}, u32[]{:S(2)}, u32[]{:S(2)}) %collective-permute-start.40) | collective-permute-done | bytes 393248 | tf_op jit(solution)/shard_map/ppermute | solution.py:68
  217.8 3.1 %collective-permute-start.41 = (bf16[1,2,16,1536]{3,2,1,0:T(8,128)(2,1)S(1)}, bf16[1,2,16,1536]{3,2,1,0:T(8,128)(2,1)S(1)}, u32[]{:S(2)}, u32[]{:S(2)}) collective-permute-start(bf16[1,2,16,1536]{3,2,1,0:T(8,128)(2,1)S(1)} %pad_maximum_fusion.7), channel_id=1, source_target_pairs={{0,64},{64,128},{128,192},{1,65},{65,129},{129,193},{2,66},{66,130... | collective-permute-start | bytes 294920 | tf_op jit(solution)/shard_map/ppermute | solution.py:73
  220.9 5.3 %collective-permute-done.42 = bf16[1,16,8,1536]{3,2,1,0:T(8,128)(2,1)S(1)} collective-permute-done((bf16[1,16,8,1536]{3,2,1,0:T(8,128)(2,1)S(1)}, bf16[1,16,8,1536]{3,2,1,0:T(8,128)(2,1)S(1)}, u32[]{:S(2)}, u32[]{:S(2)}) %collective-permute-start.42) | collective-permute-done | bytes 393248 | tf_op jit(solution)/shard_map/ppermute | solution.py:68
  226.3 2.8 %collective-permute-start.43 = (bf16[1,2,16,1536]{3,2,1,0:T(8,128)(2,1)S(1)}, bf16[1,2,16,1536]{3,2,1,0:T(8,128)(2,1)S(1)}, u32[]{:S(2)}, u32[]{:S(2)}) collective-permute-start(bf16[1,2,16,1536]{3,2,1,0:T(8,128)(2,1)S(1)} %pad_maximum_fusion.6), channel_id=1, source_target_pairs={{0,64},{64,128},{128,192},{1,65},{65,129},{129,193},{2,66},{66,130... | collective-permute-start | bytes 294920 | tf_op jit(solution)/shard_map/ppermute | solution.py:73
  229.1 1.5 collective-permute-done.43
  230.7 2.0 finish.1
  (144 shorter events, 27.4 us)
Async XLA Ops:
  1.7 16.1 %collective-permute-start.23 = (bf16[24,1536]{1,0:T(8,128)(2,1)S(1)}, bf16[24,1536]{1,0:T(8,128)(2,1)S(1)}, u32[]{:S(2)}, u32[]{:S(2)}) collective-permute-start(bf16[24,1536]{1,0:T(8,128)(2,1)S(1)} %get-tuple-element.18), channel_id=1, source_target_pairs={{0,129},{1,128},{2,131},{3,130},{4,133},{5,132},{6,135},{7,134},{8... | collective-permute-start | bytes 221192 | tf_op jit(solution)/shard_map/ppermute | solution.py:63
  5.1 11.0 %collective-permute-start.2 = (bf16[24,1536]{1,0:T(8,128)(2,1)S(1)}, bf16[24,1536]{1,0:T(8,128)(2,1)S(1)}, u32[]{:S(2)}, u32[]{:S(2)}) collective-permute-start(bf16[24,1536]{1,0:T(8,128)(2,1)S(1)} %get-tuple-element.19), channel_id=1, source_target_pairs={{0,129},{1,128},{2,131},{3,130},{4,133},{5,132},{6,135},{7,134},{8... | collective-permute-start | bytes 221192 | tf_op jit(solution)/shard_map/ppermute | solution.py:63
  6.6 77.5 %collective-permute-start = (bf16[2,16,8,1536]{3,2,1,0:T(8,128)(2,1)S(1)}, bf16[2,16,8,1536]{3,2,1,0:T(8,128)(2,1)S(1)}, u32[]{:S(2)}, u32[]{:S(2)}) collective-permute-start(bf16[2,16,8,1536]{3,2,1,0:T(8,128)(2,1)S(1)} %get-tuple-element.12), channel_id=1, source_target_pairs={{0,63},{1,0},{2,1},{3,2},{4,3},{5,4},{6,5},{7,6},{8,7},{9,8},{10,9... | collective-permute-start | bytes 2359304 | tf_op jit(solution)/shard_map/ppermute | solution.py:68
  16.3 7.3 %collective-permute-start.3 = (bf16[1,48,1536]{2,1,0:T(8,128)(2,1)S(1)}, bf16[1,48,1536]{2,1,0:T(8,128)(2,1)S(1)}, u32[]{:S(2)}, u32[]{:S(2)}) collective-permute-start(bf16[1,48,1536]{2,1,0:T(8,128)(2,1)S(1)} %maximum_bitcast_fusion), channel_id=1, source_target_pairs={{0,2},{1,3},{2,4},{3,5},{4,6},{5,7},{6,0},{7,1},{8,10},{9,11},{10,... | collective-permute-start | bytes 442376 | tf_op jit(solution)/shard_map/ppermute | solution.py:63
  17.8 28.4 %collective-permute-start.25 = (bf16[1,48,1536]{2,1,0:T(8,128)(2,1)S(1)}, bf16[1,48,1536]{2,1,0:T(8,128)(2,1)S(1)}, u32[]{:S(2)}, u32[]{:S(2)}) collective-permute-start(bf16[1,48,1536]{2,1,0:T(8,128)(2,1)S(1)} %maximum_bitcast_fusion.1), channel_id=1, source_target_pairs={{0,56},{1,57},{2,58},{3,59},{4,60},{5,61},{6,62},{7,63},{8,0},{9,1... | collective-permute-start | bytes 442376 | tf_op jit(solution)/shard_map/ppermute | solution.py:63
  23.7 43.1 %collective-permute-start.9 = (bf16[4,48,1536]{2,1,0:T(8,128)(2,1)S(1)}, bf16[4,48,1536]{2,1,0:T(8,128)(2,1)S(1)}, u32[]{:S(2)}, u32[]{:S(2)}) collective-permute-start(bf16[4,48,1536]{2,1,0:T(8,128)(2,1)S(1)} %pad_maximum_fusion.4.refs_0_), channel_id=1, source_target_pairs={{0,56},{1,57},{2,58},{3,59},{4,60},{5,61},{6,62},{7,63},{8,0},{9,1... | collective-permute-start | bytes 1769480 | tf_op jit(solution)/shard_map/ppermute | solution.py:63
  24.9 59.7 %collective-permute-start.7 = (bf16[4,48,1536]{2,1,0:T(8,128)(2,1)S(1)}, bf16[4,48,1536]{2,1,0:T(8,128)(2,1)S(1)}, u32[]{:S(2)}, u32[]{:S(2)}) collective-permute-start(bf16[4,48,1536]{2,1,0:T(8,128)(2,1)S(1)} %pad_maximum_fusion.4.refs_0_), channel_id=1, source_target_pairs={{0,8},{1,9},{2,10},{3,11},{4,12},{5,13},{6,14},{7,15},{8,16},{9,17... | collective-permute-start | bytes 1769480 | tf_op jit(solution)/shard_map/ppermute | solution.py:63
  27.5 58.2 %collective-permute-start.6 = (bf16[4,48,1536]{2,1,0:T(8,128)(2,1)S(1)}, bf16[4,48,1536]{2,1,0:T(8,128)(2,1)S(1)}, u32[]{:S(2)}, u32[]{:S(2)}) collective-permute-start(bf16[4,48,1536]{2,1,0:T(8,128)(2,1)S(1)} %pad_maximum_fusion.4.refs_0_), channel_id=1, source_target_pairs={{0,64},{1,65},{2,66},{3,67},{4,68},{5,69},{6,70},{7,71},{8,72},{9,... | collective-permute-start | bytes 1769480 | tf_op jit(solution)/shard_map/ppermute | solution.py:63
  46.2 7.1 %collective-permute-start.26 = (bf16[1,48,1536]{2,1,0:T(8,128)(2,1)S(1)}, bf16[1,48,1536]{2,1,0:T(8,128)(2,1)S(1)}, u32[]{:S(2)}, u32[]{:S(2)}) collective-permute-start(bf16[1,48,1536]{2,1,0:T(8,128)(2,1)S(1)} %collective-permute-done.24), channel_id=1, source_target_pairs={{0,8},{1,9},{2,10},{3,11},{4,12},{5,13},{6,14},{7,15},{8,16},{9,17... | collective-permute-start | bytes 442376 | tf_op jit(solution)/shard_map/ppermute | solution.py:63
  66.8 26.2 %collective-permute-start.13 = (bf16[4,48,1536]{2,1,0:T(8,128)(2,1)S(1)}, bf16[4,48,1536]{2,1,0:T(8,128)(2,1)S(1)}, u32[]{:S(2)}, u32[]{:S(2)}) collective-permute-start(bf16[4,48,1536]{2,1,0:T(8,128)(2,1)S(1)} %collective-permute-done.9.refs_4_), channel_id=1, source_target_pairs={{0,56},{1,57},{2,58},{3,59},{4,60},{5,61},{6,62},{7,63},{8,0},{9,1... | collective-permute-start | bytes 1769480 | tf_op jit(solution)/shard_map/ppermute | solution.py:63
  72.0 21.1 %collective-permute-start.10 = (bf16[4,48,1536]{2,1,0:T(8,128)(2,1)S(1)}, bf16[4,48,1536]{2,1,0:T(8,128)(2,1)S(1)}, u32[]{:S(2)}, u32[]{:S(2)}) collective-permute-start(bf16[4,48,1536]{2,1,0:T(8,128)(2,1)S(1)} %collective-permute-done.9.refs_4_), channel_id=1, source_target_pairs={{0,64},{1,65},{2,66},{3,67},{4,68},{5,69},{6,70},{7,71},{8,72},{9,... | collective-permute-start | bytes 1769480 | tf_op jit(solution)/shard_map/ppermute | solution.py:63
  84.1 27.6 %collective-permute-start.34 = (bf16[8,48,1536]{2,1,0:T(8,128)(2,1)S(1)}, bf16[8,48,1536]{2,1,0:T(8,128)(2,1)S(1)}, u32[]{:S(2)}, u32[]{:S(2)}) collective-permute-start(bf16[8,48,1536]{2,1,0:T(8,128)(2,1)S(1)} %constant_dynamic-update-slice_fusion.refs_18_), channel_id=1, source_target_pairs={{0,6},{1,7},{2,0},{3,1},{4,2},{5,3},{6,4},{7,5},{8,14},{9,15},{10,... | collective-permute-start | bytes 3538952 | tf_op jit(solution)/shard_map/ppermute | solution.py:63
  84.5 28.4 %collective-permute-start.32 = (bf16[8,48,1536]{2,1,0:T(8,128)(2,1)S(1)}, bf16[8,48,1536]{2,1,0:T(8,128)(2,1)S(1)}, u32[]{:S(2)}, u32[]{:S(2)}) collective-permute-start(bf16[8,48,1536]{2,1,0:T(8,128)(2,1)S(1)} %constant_dynamic-update-slice_fusion.refs_18_), channel_id=1, source_target_pairs={{0,2},{1,3},{2,4},{3,5},{4,6},{5,7},{6,0},{7,1},{8,10},{9,11},{10,... | collective-permute-start | bytes 3538952 | tf_op jit(solution)/shard_map/ppermute | solution.py:63
  85.7 7.3 %collective-permute-start.1 = (bf16[2,2,16,1536]{3,2,1,0:T(8,128)(2,1)S(1)}, bf16[2,2,16,1536]{3,2,1,0:T(8,128)(2,1)S(1)}, u32[]{:S(2)}, u32[]{:S(2)}) collective-permute-start(bf16[2,2,16,1536]{3,2,1,0:T(8,128)(2,1)S(1)} %pad_maximum_fusion.5), channel_id=1, source_target_pairs={{64,0},{128,64},{192,128},{65,1},{129,65},{193,129},{66,2},{130,66... | collective-permute-start | bytes 589832 | tf_op jit(solution)/shard_map/ppermute | solution.py:73
  93.0 13.7 %collective-permute-start.11 = (bf16[4,48,1536]{2,1,0:T(8,128)(2,1)S(1)}, bf16[4,48,1536]{2,1,0:T(8,128)(2,1)S(1)}, u32[]{:S(2)}, u32[]{:S(2)}) collective-permute-start(bf16[4,48,1536]{2,1,0:T(8,128)(2,1)S(1)} %collective-permute-done.7.refs_2_), channel_id=1, source_target_pairs={{0,8},{1,9},{2,10},{3,11},{4,12},{5,13},{6,14},{7,15},{8,16},{9,17... | collective-permute-start | bytes 1769480 | tf_op jit(solution)/shard_map/ppermute | solution.py:63
  93.0 13.7 %collective-permute-start.8 = (bf16[4,48,1536]{2,1,0:T(8,128)(2,1)S(1)}, bf16[4,48,1536]{2,1,0:T(8,128)(2,1)}, u32[]{:S(2)}, u32[]{:S(2)}) collective-permute-start(bf16[4,48,1536]{2,1,0:T(8,128)(2,1)S(1)} %collective-permute-done.7.refs_2_), channel_id=1, source_target_pairs={{0,64},{1,65},{2,66},{3,67},{4,68},{5,69},{6,70},{7,71},{8,72},{9,... | collective-permute-start | bytes 1769480 | tf_op jit(solution)/shard_map/ppermute | solution.py:63
  93.1 29.5 %collective-permute-start.31 = (bf16[8,48,1536]{2,1,0:T(8,128)(2,1)S(1)}, bf16[8,48,1536]{2,1,0:T(8,128)(2,1)S(1)}, u32[]{:S(2)}, u32[]{:S(2)}) collective-permute-start(bf16[8,48,1536]{2,1,0:T(8,128)(2,1)S(1)} %constant_dynamic-update-slice_fusion.refs_18_), channel_id=1, source_target_pairs={{0,64},{1,65},{2,66},{3,67},{4,68},{5,69},{6,70},{7,71},{8,72},{9,... | collective-permute-start | bytes 3538952 | tf_op jit(solution)/shard_map/ppermute | solution.py:63
  106.7 13.1 %collective-permute-start.17 = (bf16[4,48,1536]{2,1,0:T(8,128)(2,1)S(1)}, bf16[4,48,1536]{2,1,0:T(8,128)(2,1)}, u32[]{:S(2)}, u32[]{:S(2)}) collective-permute-start(bf16[4,48,1536]{2,1,0:T(8,128)(2,1)S(1)} %collective-permute-done.13.refs_8_), channel_id=1, source_target_pairs={{0,56},{1,57},{2,58},{3,59},{4,60},{5,61},{6,62},{7,63},{8,0},{9,1... | collective-permute-start | bytes 1769480 | tf_op jit(solution)/shard_map/ppermute | solution.py:63
  106.7 14.7 %collective-permute-start.15 = (bf16[4,48,1536]{2,1,0:T(8,128)(2,1)S(1)}, bf16[4,48,1536]{2,1,0:T(8,128)(2,1)S(1)}, u32[]{:S(2)}, u32[]{:S(2)}) collective-permute-start(bf16[4,48,1536]{2,1,0:T(8,128)(2,1)S(1)} %collective-permute-done.11.refs_6_), channel_id=1, source_target_pairs={{0,8},{1,9},{2,10},{3,11},{4,12},{5,13},{6,14},{7,15},{8,16},{9,17... | collective-permute-start | bytes 1769480 | tf_op jit(solution)/shard_map/ppermute | solution.py:63
  111.8 11.9 %collective-permute-start.14 = (bf16[4,48,1536]{2,1,0:T(8,128)(2,1)S(1)}, bf16[4,48,1536]{2,1,0:T(8,128)(2,1)S(1)}, u32[]{:S(2)}, u32[]{:S(2)}) collective-permute-start(bf16[4,48,1536]{2,1,0:T(8,128)(2,1)S(1)} %collective-permute-done.13.refs_8_), channel_id=1, source_target_pairs={{0,64},{1,65},{2,66},{3,67},{4,68},{5,69},{6,70},{7,71},{8,72},{9,... | collective-permute-start | bytes 1769480 | tf_op jit(solution)/shard_map/ppermute | solution.py:63
  113.0 11.2 %collective-permute-start.12 = (bf16[4,48,1536]{2,1,0:T(8,128)(2,1)S(1)}, bf16[4,48,1536]{2,1,0:T(8,128)(2,1)S(1)}, u32[]{:S(2)}, u32[]{:S(2)}) collective-permute-start(bf16[4,48,1536]{2,1,0:T(8,128)(2,1)S(1)} %collective-permute-done.11.refs_6_), channel_id=1, source_target_pairs={{0,64},{1,65},{2,66},{3,67},{4,68},{5,69},{6,70},{7,71},{8,72},{9,... | collective-permute-start | bytes 1769480 | tf_op jit(solution)/shard_map/ppermute | solution.py:63
  119.8 14.5 %collective-permute-start.38 = (bf16[8,48,768]{2,1,0:T(8,128)(2,1)S(1)}, bf16[8,48,768]{2,1,0:T(8,128)(2,1)}, u32[]{:S(2)}, u32[]{:S(2)}) collective-permute-start(bf16[8,48,768]{2,1,0:T(8,128)(2,1)S(1)} %slice.95), channel_id=1, source_target_pairs={{0,6},{1,7},{2,0},{3,1},{4,2},{5,3},{6,4},{7,5},{8,14},{9,15},{10,... | collective-permute-start | bytes 1769480 | tf_op jit(solution)/shard_map/ppermute | solution.py:63
  121.4 15.7 %collective-permute-start.36 = (bf16[8,48,768]{2,1,0:T(8,128)(2,1)S(1)}, bf16[8,48,768]{2,1,0:T(8,128)(2,1)}, u32[]{:S(2)}, u32[]{:S(2)}) collective-permute-start(bf16[8,48,768]{2,1,0:T(8,128)(2,1)S(1)} %slice.94), channel_id=1, source_target_pairs={{0,2},{1,3},{2,4},{3,5},{4,6},{5,7},{6,0},{7,1},{8,10},{9,11},{10,... | collective-permute-start | bytes 1769480 | tf_op jit(solution)/shard_map/ppermute | solution.py:63
  122.6 8.5 %collective-permute-start.21 = (bf16[4,48,768]{2,1,0:T(8,128)(2,1)S(1)}, bf16[4,48,768]{2,1,0:T(8,128)(2,1)}, u32[]{:S(2)}, u32[]{:S(2)}) collective-permute-start(bf16[4,48,768]{2,1,0:T(8,128)(2,1)S(1)} %slice.93), channel_id=1, source_target_pairs={{0,56},{1,57},{2,58},{3,59},{4,60},{5,61},{6,62},{7,63},{8,0},{9,1... | collective-permute-start | bytes 884744 | tf_op jit(solution)/shard_map/ppermute | solution.py:63
  123.6 9.7 %collective-permute-start.19 = (bf16[4,48,768]{2,1,0:T(8,128)(2,1)S(1)}, bf16[4,48,768]{2,1,0:T(8,128)(2,1)}, u32[]{:S(2)}, u32[]{:S(2)}) collective-permute-start(bf16[4,48,768]{2,1,0:T(8,128)(2,1)S(1)} %slice.92), channel_id=1, source_target_pairs={{0,8},{1,9},{2,10},{3,11},{4,12},{5,13},{6,14},{7,15},{8,16},{9,17... | collective-permute-start | bytes 884744 | tf_op jit(solution)/shard_map/ppermute | solution.py:63
  125.3 13.8 %collective-permute-start.18 = (bf16[4,48,1536]{2,1,0:T(8,128)(2,1)}, bf16[4,48,1536]{2,1,0:T(8,128)(2,1)}, u32[]{:S(2)}, u32[]{:S(2)}) collective-permute-start(bf16[4,48,1536]{2,1,0:T(8,128)(2,1)} %collective-permute-done.17.refs_12_), channel_id=1, source_target_pairs={{0,64},{1,65},{2,66},{3,67},{4,68},{5,69},{6,70},{7,71},{8,72},{9,... | collective-permute-start | bytes 1769480 | tf_op jit(solution)/shard_map/ppermute | solution.py:63
  131.2 13.2 %collective-permute-start.35 = (bf16[8,48,1536]{2,1,0:T(8,128)(2,1)}, bf16[8,48,1536]{2,1,0:T(8,128)(2,1)}, u32[]{:S(2)}, u32[]{:S(2)}) collective-permute-start(bf16[8,48,1536]{2,1,0:T(8,128)(2,1)} %copy-done.5), channel_id=1, source_target_pairs={{0,64},{1,65},{2,66},{3,67},{4,68},{5,69},{6,70},{7,71},{8,72},{9,... | collective-permute-start | bytes 3538952 | tf_op jit(solution)/shard_map/ppermute | solution.py:63
  133.3 11.1 %collective-permute-start.33 = (bf16[8,48,1536]{2,1,0:T(8,128)(2,1)}, bf16[8,48,1536]{2,1,0:T(8,128)(2,1)}, u32[]{:S(2)}, u32[]{:S(2)}) collective-permute-start(bf16[8,48,1536]{2,1,0:T(8,128)(2,1)} %copy-done.6), channel_id=1, source_target_pairs={{0,64},{1,65},{2,66},{3,67},{4,68},{5,69},{6,70},{7,71},{8,72},{9,... | collective-permute-start | bytes 3538952 | tf_op jit(solution)/shard_map/ppermute | solution.py:63
  138.0 6.4 %collective-permute-start.16 = (bf16[4,48,1536]{2,1,0:T(8,128)(2,1)}, bf16[4,48,1536]{2,1,0:T(8,128)(2,1)S(1)}, u32[]{:S(2)}, u32[]{:S(2)}) collective-permute-start(bf16[4,48,1536]{2,1,0:T(8,128)(2,1)} %copy-done.7), channel_id=1, source_target_pairs={{0,64},{1,65},{2,66},{3,67},{4,68},{5,69},{6,70},{7,71},{8,72},{9,... | collective-permute-start | bytes 1769480 | tf_op jit(solution)/shard_map/ppermute | solution.py:63
  201.4 16.4 %collective-permute-start.40 = (bf16[1,16,8,1536]{3,2,1,0:T(8,128)(2,1)S(1)}, bf16[1,16,8,1536]{3,2,1,0:T(8,128)(2,1)S(1)}, u32[]{:S(2)}, u32[]{:S(2)}) collective-permute-start(bf16[1,16,8,1536]{3,2,1,0:T(8,128)(2,1)S(1)} %get-tuple-element.16), channel_id=1, source_target_pairs={{0,1},{1,2},{2,3},{3,4},{4,5},{5,6},{6,7},{7,8},{8,9},{9,10},{10,1... | collective-permute-start | bytes 1179656 | tf_op jit(solution)/shard_map/ppermute | solution.py:68
  204.2 22.1 %collective-permute-start.42 = (bf16[1,16,8,1536]{3,2,1,0:T(8,128)(2,1)S(1)}, bf16[1,16,8,1536]{3,2,1,0:T(8,128)(2,1)S(1)}, u32[]{:S(2)}, u32[]{:S(2)}) collective-permute-start(bf16[1,16,8,1536]{3,2,1,0:T(8,128)(2,1)S(1)} %get-tuple-element.14), channel_id=1, source_target_pairs={{0,1},{1,2},{2,3},{3,4},{4,5},{5,6},{6,7},{7,8},{8,9},{9,10},{10,1... | collective-permute-start | bytes 1179656 | tf_op jit(solution)/shard_map/ppermute | solution.py:68
  217.8 11.2 %collective-permute-start.41 = (bf16[1,2,16,1536]{3,2,1,0:T(8,128)(2,1)S(1)}, bf16[1,2,16,1536]{3,2,1,0:T(8,128)(2,1)S(1)}, u32[]{:S(2)}, u32[]{:S(2)}) collective-permute-start(bf16[1,2,16,1536]{3,2,1,0:T(8,128)(2,1)S(1)} %pad_maximum_fusion.7), channel_id=1, source_target_pairs={{0,64},{64,128},{128,192},{1,65},{65,129},{129,193},{2,66},{66,130... | collective-permute-start | bytes 294920 | tf_op jit(solution)/shard_map/ppermute | solution.py:73
  (34 other events, 391.5 us)
